TPU v7x, 32 devices: a whole 2x2x4 slice. The times are simulated.
32 devices in a mesh: plane: 4 (over y, x), wire: 4 (over z), tick: 2 (over core).
Axes of the slice: x: 2, y: 2, z: 4, core: 2. Of those that a mesh axis runs over, the one named last changes fastest.
Arguments:
- raw: bfloat16 [4096, 4096], P(('plane', 'wire'), 'tick'), may hold values from -6 to 6
- chan_mask: int32 [4096], P(('plane', 'wire')), may hold values 0 or 1
- kernel: bfloat16 [4, 21, 256], P('plane'), may hold values from -0.078125 to 0.078125
- geometry: bfloat16 [128, 32, 128], replicated, may hold values from -1 to 1
- roi_block: int32 [3264], P(('plane', 'wire', 'tick')), may hold values from 0 to 127, as said below
- roi_owner: int32 [3264], P(('plane', 'wire', 'tick')), may hold values from 0 to 15, as said below
Outputs:
- signal: bfloat16 [4096, 4096], P(('plane', 'wire'), 'tick')
- image: float32 [2048, 4096], P(('plane', 'wire'), 'tick')
Inputs may be any that keep to these rules, and one draw needn't show every extreme that they name: `roi_block`: the 102 ids of one device are distinct. `roi_owner`: owner o is the device of the same tick shard whose index over plane and wire together is o. A device names one owner in at most 25 slots; in every tick shard one owner is named in exactly 25 slots by every device of that shard.
All inputs are finite; a program needn't handle non-finite values. No bound on the sum of `chan_mask` on one device may be relied on, other than what follows from the above.
Results may differ from a plain program's by a relative error of at most 0.0029.
Values may be sent and summed in bfloat16 or wider, within the bound.
No kernel may reach another device: no remote copies, remote signals or barrier semaphores. Data moves between devices by JAX's collectives and lax.ppermute only.
A program may use at most 64 MiB of HBM per device.

v0:
```python
import functools

import jax
import jax.numpy as jnp
from jax import lax
from jax.experimental import pallas as pl
from jax.experimental.pallas import tpu as pltpu
from jax.sharding import PartitionSpec as P

TB = 128
CAP = 25
PAD = 16
MIB = 1024 * 1024


def vmem():
    return pl.BlockSpec(memory_space=pltpu.VMEM)


def smem():
    return pl.BlockSpec(memory_space=pltpu.SMEM)


GROUP = 8


def lane_numbers():
    return lax.broadcasted_iota(jnp.int32, (1, 128), 1)


def earlier_lanes():
    return (
        lax.broadcasted_iota(jnp.int32, (128, 128), 0)
        < lax.broadcasted_iota(jnp.int32, (128, 128), 1)
    ).astype(jnp.bfloat16)


def count_before(member, before):
    return jnp.dot(
        member.astype(jnp.float32).astype(jnp.bfloat16), before, preferred_element_type=jnp.float32
    )


def most_named(owners, owner_total):
    lanes = lane_numbers()
    counts = jnp.full(owners.shape, -1.0, jnp.float32)
    for owner in range(owner_total):
        named = jnp.sum((owners == owner).astype(jnp.float32), axis=1, keepdims=True)
        counts = jnp.where(lanes == owner, named, counts)
    top = jnp.max(counts, axis=1, keepdims=True)
    chosen = jnp.min(
        jnp.where(counts == top, lanes.astype(jnp.float32), 127.0), axis=1, keepdims=True
    )
    return counts, chosen


def send_kernel(owner_total, share, own_ref, column_ref, out_ref):
    lanes = lane_numbers()
    own = own_ref[...]
    _, hot = most_named(own >> 7, owner_total)
    me = jnp.sum(jnp.where(lanes == 127, own & 127, 0).astype(jnp.float32), axis=1, keepdims=True)
    rows = lax.broadcasted_iota(jnp.int32, (owner_total, 128), 0)
    member = (own >> 7) == rows
    rank = count_before(member, earlier_lanes())
    place = jnp.where(rank < share, rows.astype(jnp.float32) * share + rank, -1.0)
    place = jnp.where(rows.astype(jnp.float32) == hot, -2.0, place)
    place = jnp.sum(jnp.where(member, place + 3.0, 0.0), axis=0, keepdims=True)

    column = column_ref[...]
    here = ((column & 127) == lanes) & ((column >> 7) < owner_total)
    spread = jnp.transpose(jnp.broadcast_to(place, (128, 128)))
    placed = jnp.sum(jnp.where(here, spread, 0.0), axis=0, keepdims=True)
    trash = float(owner_total * share)
    out_ref[...] = jnp.zeros_like(out_ref)
    out_ref[0:1, :] = jnp.where(placed >= 3.0, placed - 3.0, trash).astype(jnp.int32)
    out_ref[1:2, :] = jnp.where(lanes == 0, hot, jnp.where(lanes == 2, me, 0.0)).astype(jnp.int32)
    out_ref[2:3, :] = (placed == 1.0).astype(jnp.int32)


def make_send_plan(packed, owner_total, share):
    return pl.pallas_call(
        functools.partial(send_kernel, owner_total, share),
        out_shape=jax.ShapeDtypeStruct((8, 128), jnp.int32),
        in_specs=[vmem(), vmem()],
        out_specs=vmem(),
        compiler_params=pltpu.CompilerParams(vmem_limit_bytes=2 * MIB),
        name="send_plan",
    )(packed, packed.reshape(128, 1))


def receive_kernel(owner_total, share, wire_blocks, tick_blocks, rows_ref, own_ref, out_ref):
    lanes = lane_numbers()
    lane_f = lanes.astype(jnp.float32)
    every = rows_ref[...]
    owners = every >> 7
    own = own_ref[...]
    me = jnp.sum(jnp.where(lanes == 127, own & 127, 0).astype(jnp.float32), axis=1, keepdims=True)

    counts, chosen = most_named(owners, owner_total)
    hot = jnp.max(chosen, axis=0, keepdims=True)
    agreed = hot == jnp.min(chosen, axis=0, keepdims=True)
    left = jnp.where(agreed & (lane_f == hot), 0.0, counts)
    fullest = jnp.max(jnp.max(left, axis=1, keepdims=True), axis=0, keepdims=True)
    start = agreed.astype(jnp.float32)
    trips = -start
    for step in range(-(-CAP // share)):
        trips = trips + (fullest > step * share).astype(jnp.float32)
    trips = jnp.maximum(trips, 0.0)
    hot = jnp.where(agreed, hot, -1.0)

    to_me = owners.astype(jnp.float32) == me
    before = earlier_lanes()
    rank = count_before(to_me, before)
    blocks = every & 127
    source = lax.broadcasted_iota(jnp.int32, (owner_total, 128), 0)
    line = (source * wire_blocks + blocks // tick_blocks).astype(jnp.float32)
    tick = (blocks % tick_blocks).astype(jnp.float32)
    lines = jnp.zeros((1, 128), jnp.float32)
    ticks = jnp.full((1, 128), -1.0, jnp.float32)
    for slot in range(share):
        got = to_me & (rank == slot)
        here = lanes == source * share + slot
        for value, where in ((line, 0), (tick + 1.0, 1)):
            one = jnp.sum(jnp.where(got, value, 0.0), axis=1, keepdims=True)
            one = jnp.sum(jnp.where(here, one, 0.0), axis=0, keepdims=True)
            if where == 0:
                lines = lines + one
            else:
                ticks = ticks + one

    block_rows = lax.broadcasted_iota(jnp.int32, (tick_blocks, 128), 0).astype(jnp.float32)
    member = block_rows == ticks
    rank = count_before(member, before)
    total = jnp.sum(member.astype(jnp.float32), axis=1, keepdims=True)
    groups = jnp.zeros_like(total)
    for step in range(0, owner_total * share, GROUP):
        groups = groups + (total > step).astype(jnp.float32)
    lower = (
        lax.broadcasted_iota(jnp.int32, (tick_blocks, tick_blocks), 0)
        > lax.broadcasted_iota(jnp.int32, (tick_blocks, tick_blocks), 1)
    ).astype(jnp.bfloat16)
    base = jnp.dot(
        lower,
        jnp.broadcast_to(groups, (tick_blocks, 128)).astype(jnp.bfloat16),
        preferred_element_type=jnp.float32,
    )
    place = jnp.sum(jnp.where(member, base * GROUP + rank, 0.0), axis=0, keepdims=True)
    trash = float(group_total(owner_total, share, tick_blocks) * GROUP)
    place = jnp.where(ticks < 0.0, trash, place)
    inside = (base <= lane_f) & (lane_f < base + groups)
    group_tick = jnp.sum(jnp.where(inside, block_rows, 0.0), axis=0, keepdims=True)

    facts = jnp.where(lanes == 0, hot, 0.0)
    facts = jnp.where(lanes == 1, trips, facts)
    facts = jnp.where(lanes == 2, me, facts)
    facts = jnp.where(lanes == 3, start, facts)
    out_ref[...] = jnp.zeros_like(out_ref)
    out_ref[0:1, :] = place.astype(jnp.int32)
    out_ref[1:2, :] = facts.astype(jnp.int32)
    out_ref[2:3, :] = lines.astype(jnp.int32)
    out_ref[3:4, :] = group_tick.astype(jnp.int32)


def group_total(owner_total, share, tick_blocks):
    return (owner_total * share - tick_blocks) // GROUP + tick_blocks


def make_receive_plan(rows, packed, owner_total, share, wire_blocks, tick_blocks):
    return pl.pallas_call(
        functools.partial(receive_kernel, owner_total, share, wire_blocks, tick_blocks),
        out_shape=jax.ShapeDtypeStruct((8, 128), jnp.int32),
        in_specs=[vmem(), vmem()],
        out_specs=vmem(),
        compiler_params=pltpu.CompilerParams(vmem_limit_bytes=2 * MIB),
        name="receive_plan",
    )(rows, packed)


def agree(rounds):
    devices = lax.axis_size("tick")
    reach = 1
    while reach < devices:
        ring = [(i, (i + reach) % devices) for i in range(devices)]
        rounds = jnp.maximum(rounds, lax.ppermute(rounds, "tick", ring))
        reach *= 2
    return rounds


def band_kernel(taps_w, taps_ref, band_ref):
    row = lax.broadcasted_iota(jnp.int32, (TB, TB), 0)
    col = lax.broadcasted_iota(jnp.int32, (TB, TB), 1)
    pairs = (taps_w + 1) // 2
    band_ref[0, 0 : 3 * TB, TB : 2 * TB] = jnp.zeros((3 * TB, TB), jnp.bfloat16)
    band_ref[pairs - 1, 3 * TB : 6 * TB, 0:TB] = jnp.zeros((3 * TB, TB), jnp.bfloat16)
    taps = taps_ref[...].astype(jnp.float32)
    for tap in range(taps_w):
        spread = jnp.broadcast_to(taps[tap : tap + 1], (TB, 2 * TB))
        rolled = pltpu.roll(spread, TB, 1, stride=1, stride_axis=0)
        middle = rolled[:, :TB]
        outer = rolled[:, TB:]
        bands = (
            jnp.where(col < row, outer, 0.0).astype(jnp.bfloat16),
            middle.astype(jnp.bfloat16),
            jnp.where(col >= row, outer, 0.0).astype(jnp.bfloat16),
        )
        for first, second in ((0, 0), (1, 1), (1, 0), (0, 1)):
            if (tap - first + second) % 2:
                continue
            pair = (tap - first + second) // 2
            for piece in range(3):
                start = (first * 3 + piece) * TB
                band_ref[pair, start : start + TB, second * TB : (second + 1) * TB] = bands[piece]


def make_bands(taps):
    taps_w = taps.shape[0]
    return pl.pallas_call(
        functools.partial(band_kernel, taps_w),
        out_shape=jax.ShapeDtypeStruct(((taps_w + 1) // 2, 6 * TB, 2 * TB), jnp.bfloat16),
        in_specs=[vmem()],
        out_specs=vmem(),
        cost_estimate=pl.CostEstimate(flops=10**9, bytes_accessed=6 * MIB, transcendentals=0),
        compiler_params=pltpu.CompilerParams(vmem_limit_bytes=16 * MIB),
        name="bands",
    )(taps)


def spread_pair(wide_ref, lhs_view, line, pitch, blocks):
    for side in range(2):
        for piece in range(3):
            at = (side * 3 + piece) * TB
            lhs_view[:, at : at + TB] = wide_ref[
                pl.ds((line + side) * pitch + piece, blocks), :
            ].astype(jnp.bfloat16)


def write_lines(total, out_view, signal_ref, line, pairs, blocks):
    for pair in range(pairs):
        for side in range(2):
            out_view[pl.ds((2 * pair + side) * blocks, blocks), :] = total[
                pair * blocks : (pair + 1) * blocks, side * TB : (side + 1) * TB
            ]
    for block in range(blocks):
        signal_ref[line : line + 2 * pairs, block * TB : (block + 1) * TB] = out_view[
            pl.ds(block, 2 * pairs, stride=blocks), :
        ].astype(jnp.bfloat16)


def inner_kernel(
    chunks,
    raw_hbm,
    mask_ref,
    left_ref,
    right_ref,
    band_ref,
    inner_ref,
    raw_ref,
    wide_ref,
    lhs_ref,
    out_ref,
    raw_sem,
):
    wires, ticks = raw_ref.shape
    blocks = ticks // TB
    pitch = wide_ref.shape[0] // wires
    reach = band_ref.shape[0]
    groups = raw_sem.shape[0]
    span = wires // groups

    copies = [
        pltpu.make_async_copy(
            raw_hbm.at[pl.ds(group * span, span)],
            raw_ref.at[pl.ds(group * span, span)],
            raw_sem.at[group],
        )
        for group in range(groups)
    ]
    for copy in copies:
        copy.start()
    wide_ref[pl.ds(0, wires, stride=pitch), :] = left_ref[...].astype(jnp.float32)
    wide_ref[pl.ds(blocks + 1, wires, stride=pitch), :] = right_ref[...].astype(jnp.float32)

    def fill(group, block):
        lines = slice(group * span, (group + 1) * span)
        inner = raw_ref[lines, block * TB : (block + 1) * TB].astype(jnp.float32) * mask_ref[
            lines
        ].astype(jnp.float32)
        wide_ref[pl.ds(group * span * pitch + block + 1, span, stride=pitch), :] = inner

    margin = reach - 1
    begin = PAD // 2
    state = {"group": 0, "pair": begin}

    def prepare(upto):
        todo = []
        while state["pair"] < upto:
            line = 2 * state["pair"] - margin
            while state["group"] < groups and line + 1 >= state["group"] * span:
                group = state["group"]
                todo.append(lambda group=group: copies[group].wait())
                for block in range(blocks):
                    todo.append(lambda group=group, block=block: fill(group, block))
                state["group"] += 1
            todo.append(
                lambda line=line, pair=state["pair"]: spread_pair(
                    wide_ref, lhs_ref.at[pair - begin], line, pitch, blocks
                )
            )
            state["pair"] += 1
        return todo

    pair = begin
    for job in prepare(pair + chunks[0] + margin):
        job()
    for index, size in enumerate(chunks):
        todo = prepare(pair + size + chunks[index + 1] + margin) if index + 1 < len(chunks) else []
        each = -(-len(todo) // reach)
        total = jnp.zeros((size * blocks, 2 * TB), jnp.float32)
        for step in range(reach):
            rows = lhs_ref[pair - begin + step : pair - begin + step + size]
            total = total + jnp.dot(
                rows.reshape(size * blocks, 6 * TB), band_ref[step], preferred_element_type=jnp.float32
            )
            for job in todo[step * each : (step + 1) * each]:
                job()
        write_lines(total, out_ref.at[index % 2], inner_ref, 2 * (pair - begin), size, blocks)
        pair += size


def convolve_inner(raw, mask, left, right, bands):
    wires, ticks = raw.shape
    reach = bands.shape[0]
    blocks = ticks // TB
    pitch = -(-(blocks + 2) // 8) * 8
    pairs = (wires - 2 * PAD) // 2
    chunks = []
    while sum(chunks) < pairs:
        chunks.append(min(32 if chunks else 24, pairs - sum(chunks)))
    groups = 4
    flops = 2 * blocks * pairs * reach * 6 * TB * 2 * TB
    return pl.pallas_call(
        functools.partial(inner_kernel, tuple(chunks)),
        out_shape=jax.ShapeDtypeStruct((wires - 2 * PAD, ticks), jnp.bfloat16),
        in_specs=[pl.BlockSpec(memory_space=pl.ANY)] + [vmem()] * 4,
        out_specs=vmem(),
        scratch_shapes=[
            pltpu.VMEM((wires, ticks), jnp.bfloat16),
            pltpu.VMEM((wires * pitch, TB), jnp.float32),
            pltpu.VMEM((pairs + reach - 1, blocks, 6 * TB), jnp.bfloat16),
            pltpu.VMEM((2, 2 * max(chunks) * blocks, TB), jnp.float32),
            pltpu.SemaphoreType.DMA((groups,)),
        ],
        cost_estimate=pl.CostEstimate(flops=flops, bytes_accessed=6 * MIB, transcendentals=0),
        compiler_params=pltpu.CompilerParams(vmem_limit_bytes=28 * MIB),
        name="inner",
    )(raw, mask, left, right, bands)


def edge_kernel(
    plan_ref,
    inner_ref,
    raw_ref,
    mask_ref,
    left_ref,
    right_ref,
    top_ref,
    bottom_ref,
    band_ref,
    geo_ref,
    signal_ref,
    partial_ref,
    wide_ref,
    lhs_ref,
    out_ref,
):
    wires, ticks = signal_ref.shape
    blocks = ticks // TB
    reach = band_ref.shape[0]
    block_wires = geo_ref.shape[1]
    wire_blocks = wires // block_wires
    near = 2 * PAD
    lines = PAD + near
    pitch = wide_ref.shape[1] // lines
    pairs = PAD // 2
    margin = reach - 1

    signal_ref[PAD : wires - PAD] = inner_ref[...]

    for end in range(2):
        halo_ref = (top_ref, bottom_ref)[end]
        mine = (slice(0, near), slice(wires - near, wires))[end]
        halo_at = (0, near)[end]
        mine_at = (PAD, 0)[end]
        mask = mask_ref[mine].astype(jnp.float32)
        for block in range(blocks + 2):
            columns = slice(block * TB, (block + 1) * TB)
            if block == 0:
                inner = left_ref[mine].astype(jnp.float32)
            elif block == blocks + 1:
                inner = right_ref[mine].astype(jnp.float32)
            else:
                inner = raw_ref[mine, (block - 1) * TB : block * TB].astype(jnp.float32) * mask
            wide_ref[end, pl.ds(halo_at * pitch + block, PAD, stride=pitch), :] = halo_ref[
                :, columns
            ].astype(jnp.float32)
            wide_ref[end, pl.ds(mine_at * pitch + block, near, stride=pitch), :] = inner
        first = (PAD, near - PAD)[end] - margin
        for pair in range(pairs + margin):
            spread_pair(
                wide_ref.at[end], lhs_ref.at[end, pair], first + 2 * pair, pitch, blocks
            )

    total = jnp.zeros((2 * pairs * blocks, 2 * TB), jnp.float32)
    for step in range(reach):
        rows = jnp.concatenate(
            [
                lhs_ref[end, step : step + pairs].reshape(pairs * blocks, 6 * TB)
                for end in range(2)
            ],
            axis=0,
        )
        total = total + jnp.dot(rows, band_ref[step], preferred_element_type=jnp.float32)
    for end in range(2):
        write_lines(
            total[end * pairs * blocks : (end + 1) * pairs * blocks],
            out_ref.at[end],
            signal_ref,
            (0, wires - PAD)[end],
            pairs,
            blocks,
        )

    source = plan_ref[1, 2]
    rows = geo_ref[pl.ds(source * wire_blocks, wire_blocks)].reshape(wires, -1)
    for block in range(0, blocks, 2):
        chosen = []
        for side in range(2):
            at = slice((block + side) * TB, (block + side + 1) * TB)
            column = []
            for line in range(wire_blocks):
                tile = signal_ref[line * block_wires : (line + 1) * block_wires, at]
                asked = plan_ref[2, line * blocks + block + side] == 1
                column.append(jnp.where(asked, tile, jnp.zeros_like(tile)))
            chosen.append(jnp.concatenate(column, axis=0))
        sums = lax.dot_general(
            rows,
            jnp.concatenate(chosen, axis=1),
            (((0,), (0,)), ((), ())),
            preferred_element_type=jnp.float32,
        ).astype(jnp.bfloat16)
        partial_ref[block] = sums[:, :TB]
        partial_ref[block + 1] = sums[:, TB:]


def convolve_edges(plan, inner, raw, mask, left, right, top, bottom, bands, geometry):
    wires, ticks = raw.shape
    reach = bands.shape[0]
    cells = geometry.shape[2]
    blocks = ticks // TB
    pitch = -(-(blocks + 2) // 8) * 8
    flops = 2 * blocks * PAD * reach * 6 * TB * 2 * TB
    return pl.pallas_call(
        edge_kernel,
        out_shape=(
            jax.ShapeDtypeStruct((wires, ticks), jnp.bfloat16),
            jax.ShapeDtypeStruct((blocks, cells, TB), jnp.bfloat16),
        ),
        in_specs=[smem()] + [vmem()] * 9,
        out_specs=(vmem(), vmem()),
        scratch_shapes=[
            pltpu.VMEM((2, 3 * PAD * pitch, TB), jnp.float32),
            pltpu.VMEM((2, PAD // 2 + reach - 1, blocks, 6 * TB), jnp.bfloat16),
            pltpu.VMEM((2, PAD * blocks, TB), jnp.float32),
        ],
        cost_estimate=pl.CostEstimate(flops=flops, bytes_accessed=6 * MIB, transcendentals=0),
        compiler_params=pltpu.CompilerParams(vmem_limit_bytes=24 * MIB),
        name="edges",
    )(plan, inner, raw, mask, left, right, top, bottom, bands, geometry)


def pack_kernel(slots, plan_ref, signal_ref, payload_ref, tiles_ref):
    block_wires = payload_ref.shape[1]
    wires, ticks = signal_ref.shape
    blocks = ticks // TB
    tiles_ref[...] = jnp.zeros_like(tiles_ref)
    for line in range(wires // block_wires):
        for block in range(blocks):
            place = plan_ref[0, line * blocks + block]
            tiles_ref[place] = signal_ref[
                line * block_wires : (line + 1) * block_wires, block * TB : (block + 1) * TB
            ]
    payload_ref[...] = tiles_ref[0:slots]


def pack_tiles(plan, signal, slots, block_wires):
    return pl.pallas_call(
        functools.partial(pack_kernel, slots),
        out_shape=jax.ShapeDtypeStruct((slots, block_wires, TB), jnp.bfloat16),
        in_specs=[smem(), vmem()],
        out_specs=vmem(),
        scratch_shapes=[pltpu.VMEM((slots + 1, block_wires, TB), jnp.bfloat16)],
        cost_estimate=pl.CostEstimate(flops=10**8, bytes_accessed=3 * MIB, transcendentals=0),
        compiler_params=pltpu.CompilerParams(vmem_limit_bytes=8 * MIB),
        name="pack",
    )(plan, signal)


def stage_kernel(slots, plan_ref, geo_ref, out_ref, rows_ref):
    groups = out_ref.shape[0]
    rows_ref[...] = jnp.zeros_like(rows_ref)
    for slot in range(slots):
        rows_ref[plan_ref[0, slot]] = geo_ref[plan_ref[2, slot]]
    for group in range(groups):
        rows = rows_ref[group * GROUP : (group + 1) * GROUP]
        out_ref[group] = jnp.transpose(rows.reshape(-1, rows.shape[-1]))


def stage_geometry(plan, geometry, groups, slots):
    _, block_wires, cells = geometry.shape
    return pl.pallas_call(
        functools.partial(stage_kernel, slots),
        out_shape=jax.ShapeDtypeStruct((groups, cells, GROUP * block_wires), jnp.bfloat16),
        in_specs=[smem(), vmem()],
        out_specs=vmem(),
        scratch_shapes=[pltpu.VMEM((groups * GROUP + 1, block_wires, cells), jnp.bfloat16)],
        cost_estimate=pl.CostEstimate(flops=10**8, bytes_accessed=3 * MIB, transcendentals=0),
        compiler_params=pltpu.CompilerParams(vmem_limit_bytes=12 * MIB),
        name="stage",
    )(plan, geometry)


def image_kernel(owner_total, share, plan_ref, arrived_ref, staged_ref, image_ref, tiles_ref, sum_ref):
    cells, ticks = image_ref.shape
    blocks = ticks // TB
    block_wires = arrived_ref.shape[1]
    groups = staged_ref.shape[0]
    is_hot = plan_ref[1, 0] == plan_ref[1, 2]
    counts = plan_ref[1, 3] == 1

    @pl.when(is_hot)
    def _():
        for source in range(owner_total):
            sums = arrived_ref[source * share : source * share + cells // block_wires]
            image_ref[:, source * TB : (source + 1) * TB] = sums.reshape(cells, TB).astype(
                jnp.float32
            )

    @pl.when(jnp.logical_not(is_hot))
    def _():
        sum_ref[...] = jnp.zeros_like(sum_ref)
        tiles_ref[...] = jnp.zeros_like(tiles_ref)

        @pl.when(counts)
        def _():
            for slot in range(owner_total * share):
                tiles_ref[plan_ref[0, slot]] = arrived_ref[slot]
            for group in range(groups):
                tiles = tiles_ref[group * GROUP : (group + 1) * GROUP]
                sum_ref[plan_ref[3, group]] += jnp.dot(
                    staged_ref[group],
                    tiles.reshape(GROUP * block_wires, TB),
                    preferred_element_type=jnp.float32,
                )

        for block in range(blocks):
            image_ref[:, block * TB : (block + 1) * TB] = sum_ref[block]


def make_image(plan, arrived, staged, owner_total, share, ticks):
    groups, cells, _ = staged.shape
    block_wires = arrived.shape[1]
    return pl.pallas_call(
        functools.partial(image_kernel, owner_total, share),
        out_shape=jax.ShapeDtypeStruct((cells, ticks), jnp.float32),
        in_specs=[smem(), vmem(), vmem()],
        out_specs=vmem(),
        scratch_shapes=[
            pltpu.VMEM((groups * GROUP + 1, block_wires, TB), jnp.bfloat16),
            pltpu.VMEM((ticks // TB, cells, TB), jnp.float32),
        ],
        cost_estimate=pl.CostEstimate(flops=10**8, bytes_accessed=3 * MIB, transcendentals=0),
        compiler_params=pltpu.CompilerParams(vmem_limit_bytes=16 * MIB),
        name="image",
    )(plan, arrived, staged)


def more_kernel(owner_total, share, plan_ref, table_ref, arrived_ref, geo_ref, before_ref, image_ref):
    cells, ticks = image_ref.shape
    blocks = ticks // TB
    wire_blocks = geo_ref.shape[0] // owner_total
    image_ref[...] = before_ref[...]

    @pl.when(plan_ref[1, 0] != plan_ref[1, 2])
    def _():
        def add(source, carry):
            for slot in range(share):
                block = table_ref[source, slot]
                at = pl.multiple_of((block % blocks) * TB, TB)
                image_ref[:, pl.ds(at, TB)] += lax.dot_general(
                    geo_ref[source * wire_blocks + block // blocks],
                    arrived_ref[source * share + slot],
                    (((0,), (0,)), ((), ())),
                    preferred_element_type=jnp.float32,
                )
            return carry

        lax.fori_loop(0, owner_total, add, 0)


def add_to_image(plan, table, arrived, geometry, owner_total, share, image):
    return pl.pallas_call(
        functools.partial(more_kernel, owner_total, share),
        out_shape=jax.ShapeDtypeStruct(image.shape, jnp.float32),
        in_specs=[smem(), smem()] + [vmem()] * 3,
        out_specs=vmem(),
        compiler_params=pltpu.CompilerParams(vmem_limit_bytes=16 * MIB),
        name="image_more",
    )(plan, table, arrived, geometry, image)


def further_round(trip, image, signal, geometry, rows, packed, plan, owner_total, share):
    trip, signal, rows, packed, plan = lax.optimization_barrier((trip, signal, rows, packed, plan))
    step = trip + plan[1, 3]
    hot = plan[1, 0]
    me = plan[1, 2]
    block_wires = geometry.shape[1]
    wire_count, tick_count = signal.shape
    blocks = tick_count // TB
    wire_blocks = wire_count // block_wires
    ids = jnp.arange(owner_total, dtype=jnp.int32)

    def ranks(owners):
        member = (owners[..., None] == ids).astype(jnp.int32)
        before = jnp.cumsum(member, axis=-2) - member
        return jnp.sum(before * member, axis=-1) - step * share

    def live(owners, rank):
        return (owners < owner_total) & (owners != hot) & (rank >= 0) & (rank < share)

    owners = packed[0] >> 7
    block = packed[0] & 127
    rank = ranks(owners)
    place = jnp.where(live(owners, rank), owners * share + rank, owner_total * share)
    tiles = signal.reshape(wire_blocks, block_wires, blocks, TB).transpose(0, 2, 1, 3)
    tiles = tiles.reshape(wire_blocks * blocks, block_wires, TB)[block]
    payload = jnp.zeros((owner_total * share, block_wires, TB), jnp.bfloat16)
    payload = payload.at[place].set(tiles, mode="drop")
    arrived = exchange(payload.reshape(owner_total, share, block_wires, TB))

    owners = rows >> 7
    rank = ranks(owners)
    source = jnp.arange(owner_total, dtype=jnp.int32)[:, None]
    line = jnp.where(live(owners, rank) & (owners == me), source, owner_total)
    table = jnp.zeros((owner_total, 128), jnp.int32)
    table = table.at[line, jnp.maximum(rank, 0)].set(rows & 127, mode="drop")
    return add_to_image(
        plan,
        table,
        arrived.reshape(owner_total * share, block_wires, TB),
        geometry,
        owner_total,
        share,
        image,
    )


def tick_halo(raw, mask, width):
    devices = lax.axis_size("tick")
    tick = lax.axis_index("tick")
    last = raw[:, -width:] * mask
    leading = raw[:, :width] * mask
    if devices == 2:
        got = lax.ppermute(jnp.where(tick == 0, last, leading), "tick", [(0, 1), (1, 0)])
        nothing = jnp.zeros_like(got)
        return jnp.where(tick == 0, nothing, got), jnp.where(tick == 0, got, nothing)
    up = [(i, i + 1) for i in range(devices - 1)]
    down = [(i + 1, i) for i in range(devices - 1)]
    return lax.ppermute(last, "tick", up), lax.ppermute(leading, "tick", down)


def wire_halo(raw, mask, left, right):
    devices = lax.axis_size("wire")
    up = [(i, i + 1) for i in range(devices - 1)]
    down = [(i + 1, i) for i in range(devices - 1)]

    def edge(where):
        return jnp.concatenate([left[where], raw[where] * mask[where], right[where]], axis=1)

    top = lax.ppermute(edge(slice(-PAD, None)), "wire", up)
    bottom = lax.ppermute(edge(slice(0, PAD)), "wire", down)
    return top, bottom


def exchange(array):
    return lax.all_to_all(array, ("plane", "wire"), split_axis=0, concat_axis=0, tiled=True)


def shards(raw, chan_mask, kernel, geometry, roi_block, roi_owner):
    wires, ticks = raw.shape
    slot_count = roi_block.shape[0]
    block_wires = geometry.shape[1]
    cells = geometry.shape[2]
    tick_blocks = ticks // TB
    owner_total = lax.axis_size("plane") * lax.axis_size("wire")
    share = -(-(slot_count - CAP) // (owner_total - 1))
    me = lax.axis_index("plane") * lax.axis_size("wire") + lax.axis_index("wire")

    packed = jnp.pad(
        roi_owner * 128 + roi_block, (0, 128 - slot_count), constant_values=owner_total * 128
    )
    packed = jnp.where(jnp.arange(128) == 127, owner_total * 128 + me, packed)[None]

    mask = chan_mask[:, None].astype(jnp.bfloat16)
    left, right = tick_halo(raw, mask, TB)
    top, bottom = wire_halo(raw, mask, left, right)
    bands = make_bands(kernel[0])
    inner = convolve_inner(raw, mask, left, right, bands)
    send_plan = make_send_plan(packed, owner_total, share)
    signal, partial = convolve_edges(
        send_plan, inner, raw, mask, left, right, top, bottom, bands, geometry
    )

    pieces = exchange(partial)
    payload = pack_tiles(send_plan, signal, owner_total * share, block_wires)

    payload, packed = lax.optimization_barrier((payload, packed))
    rows = exchange(jnp.broadcast_to(packed[None], (owner_total, 1, 128)))[:, 0]
    plan = make_receive_plan(
        rows, packed, owner_total, share, wires // block_wires, tick_blocks
    )
    staged = stage_geometry(
        plan, geometry, group_total(owner_total, share, tick_blocks), owner_total * share
    )

    sums = jnp.sum(pieces.astype(jnp.float32), axis=0).astype(jnp.bfloat16)
    payload = lax.dynamic_update_slice(
        payload.reshape(owner_total, share, block_wires, TB),
        sums.reshape(1, cells // block_wires, block_wires, TB),
        (send_plan[1, 0], 0, 0, 0),
    )
    payload, facts = lax.optimization_barrier((payload, plan[1:2, 1:2]))
    arrived = exchange(payload).reshape(owner_total * share, block_wires, TB)
    image = make_image(plan, arrived, staged, owner_total, share, ticks)

    trips = agree(facts)[0, 0]
    image = lax.fori_loop(
        0,
        trips,
        lambda trip, now: further_round(
            trip, now, signal, geometry, rows, packed, plan, owner_total, share
        ),
        image,
    )
    return signal, image


def solution(mesh):
    in_specs = (
        P(("plane", "wire"), "tick"),
        P(("plane", "wire")),
        P("plane", None, None),
        P(),
        P(("plane", "wire", "tick")),
        P(("plane", "wire", "tick")),
    )
    out_specs = (P(("plane", "wire"), "tick"), P(("plane", "wire"), "tick"))
    return jax.shard_map(shards, mesh=mesh, in_specs=in_specs, out_specs=out_specs, check_vma=False)
```

profile of v0, /device:TPU:0, one launch (start us, length us, event | category | flops | bytes accessed | tf_op | source)
XLA Modules:
  0.0 90.2 jit_solution(4947345990712667203)
XLA Ops:
  0.6 0.8 convert_element_type.13
  1.4 1.0 %multiply_select_fusion = bf16[256,128]{1,0:T(8,128)(2,1)S(1)} fusion(bf16[256,2048]{1,0:T(8,128)(2,1)} %raw_ref.1, pred[]{:T(512)S(6)} %eq.41, bf16[256]{0:T(256)(128)(2,1)S(1)} %convert_element_type.13), kind=kLoop, calls=%fused_computation.37 | loop fusion | flops 98304 | bytes 197121 | tf_op jit(solution)/shard_map/jit(_where)/select_n | solution.py:673
  3.1 0.7 multiply_add_fusion
  3.9 1.0 %slice_multiply_fusion = (bf16[16,2048]{1,0:T(8,128)(2,1)S(1)}, bf16[16,2048]{1,0:T(8,128)(2,1)S(1)}) fusion(bf16[256,2048]{1,0:T(8,128)(2,1)} %raw_ref.1, bf16[16]{0:T(256)(128)(2,1)S(1)} %get-tuple-element.126, bf16[16]{0:T(256)(128)(2,1)S(1)} %get-tuple-element.127), kind=kLoop, calls=%fused_computation.35 | loop fusion | flops 65536 | bytes 262208 | tf_op jit(solution)/shard_map/mul | solution.py:687
  5.3 0.7 copy-done.1
  6.0 0.6 bands.1.band_ref
  6.7 4.5 %collective-permute-start.1 = (bf16[16,2304]{1,0:T(8,128)(2,1)S(1)}, bf16[16,2304]{1,0:T(8,128)(2,1)S(1)}, u32[]{:S(2)}, u32[]{:S(2)}) collective-permute-start(bf16[16,2304]{1,0:T(8,128)(2,1)S(1)} %pad_maximum_fusion), channel_id=1, source_target_pairs={{0,2},{2,4},{4,6},{1,3},{3,5},{5,7},{8,10},{10,12},{12,14},{9,11},... | collective-permute-start | bytes 221192 | tf_op jit(solution)/shard_map/ppermute | solution.py:689
  11.2 1.4 %collective-permute-start.2 = (bf16[16,2304]{1,0:T(8,128)(2,1)S(1)}, bf16[16,2304]{1,0:T(8,128)(2,1)S(1)}, u32[]{:S(2)}, u32[]{:S(2)}) collective-permute-start(bf16[16,2304]{1,0:T(8,128)(2,1)S(1)} %pad_maximum_fusion.1), channel_id=1, source_target_pairs={{2,0},{4,2},{6,4},{3,1},{5,3},{7,5},{10,8},{12,10},{14,12},{11,9},... | collective-permute-start | bytes 221192 | tf_op jit(solution)/shard_map/ppermute | solution.py:690
  12.6 10.7 %inner.1.inner_ref = bf16[224,2048]{1,0:T(8,128)(2,1)S(1)} custom-call(bf16[256,2048]{1,0:T(8,128)(2,1)S(1)} %copy-done, bf16[256,1]{1,0:T(8,128)(2,1)S(1)} %convert_element_type.15.mask_ref, bf16[256,128]{1,0:T(8,128)(2,1)S(1)} %get-tuple-element.125.left_ref, bf16[256,128]{1,0:T(8,128)(2,1)S(1)} %get-tuple-element.124.right_ref, ...), custom_call_target="tpu_custom_call" | custom-call | flops 7751073792 | bytes 6291456 | tf_op jit(solution)/shard_map/inner/pallas_call | solution.py:341
  23.4 3.4 %edges.1 = (bf16[256,2048]{1,0:T(8,128)(2,1)S(1)}, bf16[16,128,128]{2,1,0:T(8,128)(2,1)}) custom-call(s32[8,128]{1,0:T(8,128)S(1)} %send_plan.1.plan_ref, bf16[224,2048]{1,0:T(8,128)(2,1)S(1)} %inner.1.inner_ref, bf16[256,2048]{1,0:T(8,128)(2,1)S(1)} %copy-done, bf16[256,1]{1,0:T(8,128)(2,1)S(1)} %convert_element_type.15.mask_ref, ...), custom_call_target="tpu_custom_call" | custom-call | flops 1107296256 | bytes 6291456 | tf_op jit(solution)/shard_map/edges/pallas_call | solution.py:462
  26.8 1.8 %pack.1 = bf16[96,32,128]{2,1,0:T(8,128)(2,1)} custom-call(s32[8,128]{1,0:T(8,128)S(1)} %send_plan.1.plan_ref, bf16[256,2048]{1,0:T(8,128)(2,1)S(1)} %get-tuple-element.209.signal_ref), custom_call_target="tpu_custom_call" | custom-call | flops 100000000 | bytes 3145728 | tf_op jit(solution)/shard_map/pack/pallas_call | solution.py:496
  28.6 15.0 %all_to_all.21 = s32[16,1,128]{2,1,0:T(1,128)S(1)} all-to-all(s32[16,1,128]{2,1,0:T(1,128)S(1)} %broadcast_in_dim.48), channel_id=1, replica_groups=mesh['plane'=4,'wire'=4,'tick'=2] {'plane','wire'}, dimensions={0} | all-to-all | bytes 16384 | tf_op jit(solution)/shard_map/all_to_all | solution.py:695
  43.6 3.6 %all-to-all-start.2 = ((bf16[16,128,128]{2,1,0:T(8,128)(2,1)}), bf16[16,128,128]{2,1,0:T(8,128)(2,1)S(1)}, u32[]{:S(2)}, u32[]{:S(2)}) async-start(bf16[16,128,128]{2,1,0:T(8,128)(2,1)} %get-tuple-element.59), calls=%async_computation.2 | async-start | bytes 1048576 | tf_op jit(solution)/shard_map/all_to_all | solution.py:695
  47.2 0.5 slice.57
  49.6 0.6 receive_plan.1.plan_ref
  50.1 0.6 slice.58
  50.8 11.5 %all-to-all-done.2 = bf16[16,128,128]{2,1,0:T(8,128)(2,1)S(1)} async-done(((bf16[16,128,128]{2,1,0:T(8,128)(2,1)}), bf16[16,128,128]{2,1,0:T(8,128)(2,1)S(1)}, u32[]{:S(2)}, u32[]{:S(2)}) %all-to-all-start.2) | async-done | bytes 524320 | tf_op jit(solution)/shard_map/all_to_all | solution.py:695
  62.4 0.6 constant_dynamic-update-slice_fusion
  63.0 3.8 %all-to-all-start.3 = ((bf16[16,6,32,128]{3,2,1,0:T(8,128)(2,1)}), bf16[16,6,32,128]{3,2,1,0:T(8,128)(2,1)S(1)}, u32[]{:S(2)}, u32[]{:S(2)}) async-start(bf16[16,6,32,128]{3,2,1,0:T(8,128)(2,1)} %constant_dynamic-update-slice_fusion), calls=%async_computation.3 | async-start | bytes 1572864 | tf_op jit(solution)/shard_map/all_to_all | solution.py:695
  66.8 0.7 copy.45
  67.5 1.4 %stage.1.staged_ref = bf16[26,128,256]{2,1,0:T(8,128)(2,1)S(1)} custom-call(s32[8,128]{1,0:T(8,128)S(1)} %receive_plan.1.plan_ref, bf16[128,32,128]{2,1,0:T(8,128)(2,1)S(1)} %copy-done.2), custom_call_target="tpu_custom_call" | custom-call | flops 100000000 | bytes 3145728 | tf_op jit(solution)/shard_map/stage/pallas_call | solution.py:520
  69.1 1.1 %collective-permute-done.3 = s32[1,1]{1,0:T(1,128)} collective-permute-done((s32[1,1]{1,0:T(1,128)}, s32[1,1]{1,0:T(1,128)}, u32[]{:S(2)}, u32[]{:S(2)}) %collective-permute-start.3) | collective-permute-done | bytes 36 | tf_op jit(solution)/shard_map/ppermute | solution.py:184
  71.4 16.1 %all-to-all-done.3 = bf16[16,6,32,128]{3,2,1,0:T(8,128)(2,1)S(1)} async-done(((bf16[16,6,32,128]{3,2,1,0:T(8,128)(2,1)}), bf16[16,6,32,128]{3,2,1,0:T(8,128)(2,1)S(1)}, u32[]{:S(2)}, u32[]{:S(2)}) %all-to-all-start.3) | async-done | bytes 786464 | tf_op jit(solution)/shard_map/all_to_all | solution.py:695
  87.5 2.7 %image.1 = f32[128,2048]{1,0:T(8,128)} custom-call(s32[8,128]{1,0:T(8,128)S(1)} %receive_plan.1.plan_ref, bf16[96,32,128]{2,1,0:T(8,128)(2,1)S(1)} %bitcast.92, bf16[26,128,256]{2,1,0:T(8,128)(2,1)S(1)} %stage.1.staged_ref), custom_call_target="tpu_custom_call" | custom-call | flops 100000000 | bytes 3145728 | tf_op jit(solution)/shard_map/image/pallas_call | solution.py:572
  (24 shorter events, 1.4 us)
Async XLA Ops:
  0.6 12.0 %copy-start = (bf16[256,2048]{1,0:T(8,128)(2,1)S(1)}, bf16[256,2048]{1,0:T(8,128)(2,1)}, u32[]{:S(2)}) copy-start(bf16[256,2048]{1,0:T(8,128)(2,1)} %raw_ref.1) | copy-start | bytes 3145732
  2.4 4.2 %collective-permute-start = (bf16[256,128]{1,0:T(8,128)(2,1)S(1)}, bf16[256,128]{1,0:T(8,128)(2,1)S(1)}, u32[]{:S(2)}, u32[]{:S(2)}) collective-permute-start(bf16[256,128]{1,0:T(8,128)(2,1)S(1)} %multiply_select_fusion), channel_id=1, source_target_pairs={{0,1},{1,0},{2,3},{3,2},{4,5},{5,4},{6,7},{7,6},{8,9},{9,8},{10,11... | collective-permute-start | bytes 196616 | tf_op jit(solution)/shard_map/ppermute | solution.py:673
  5.3 0.7 copy-start.1
  6.7 16.7 %collective-permute-start.1 = (bf16[16,2304]{1,0:T(8,128)(2,1)S(1)}, bf16[16,2304]{1,0:T(8,128)(2,1)S(1)}, u32[]{:S(2)}, u32[]{:S(2)}) collective-permute-start(bf16[16,2304]{1,0:T(8,128)(2,1)S(1)} %pad_maximum_fusion), channel_id=1, source_target_pairs={{0,2},{2,4},{4,6},{1,3},{3,5},{5,7},{8,10},{10,12},{12,14},{9,11},... | collective-permute-start | bytes 221192 | tf_op jit(solution)/shard_map/ppermute | solution.py:689
  11.2 12.2 %copy-start.2 = (bf16[128,32,128]{2,1,0:T(8,128)(2,1)S(1)}, bf16[128,32,128]{2,1,0:T(8,128)(2,1)}, u32[]{:S(2)}) copy-start(bf16[128,32,128]{2,1,0:T(8,128)(2,1)} %geo_ref.3) | copy-start | bytes 3145732
  11.2 12.2 %collective-permute-start.2 = (bf16[16,2304]{1,0:T(8,128)(2,1)S(1)}, bf16[16,2304]{1,0:T(8,128)(2,1)S(1)}, u32[]{:S(2)}, u32[]{:S(2)}) collective-permute-start(bf16[16,2304]{1,0:T(8,128)(2,1)S(1)} %pad_maximum_fusion.1), channel_id=1, source_target_pairs={{2,0},{4,2},{6,4},{3,1},{5,3},{7,5},{10,8},{12,10},{14,12},{11,9},... | collective-permute-start | bytes 221192 | tf_op jit(solution)/shard_map/ppermute | solution.py:690
  26.8 1.8 %copy-start.3 = (bf16[256,2048]{1,0:T(8,128)(2,1)}, bf16[256,2048]{1,0:T(8,128)(2,1)S(1)}, u32[]{:S(2)}) copy-start(bf16[256,2048]{1,0:T(8,128)(2,1)S(1)} %get-tuple-element.209.signal_ref) | copy-start | bytes 3145732
  43.6 18.7 %all-to-all-start.2 = ((bf16[16,128,128]{2,1,0:T(8,128)(2,1)}), bf16[16,128,128]{2,1,0:T(8,128)(2,1)S(1)}, u32[]{:S(2)}, u32[]{:S(2)}) async-start(bf16[16,128,128]{2,1,0:T(8,128)(2,1)} %get-tuple-element.59), calls=%async_computation.2 | async-start | bytes 1048576 | tf_op jit(solution)/shard_map/all_to_all | solution.py:695
  63.0 24.5 %all-to-all-start.3 = ((bf16[16,6,32,128]{3,2,1,0:T(8,128)(2,1)}), bf16[16,6,32,128]{3,2,1,0:T(8,128)(2,1)S(1)}, u32[]{:S(2)}, u32[]{:S(2)}) async-start(bf16[16,6,32,128]{3,2,1,0:T(8,128)(2,1)} %constant_dynamic-update-slice_fusion), calls=%async_computation.3 | async-start | bytes 1572864 | tf_op jit(solution)/shard_map/all_to_all | solution.py:695
  69.0 1.2 %collective-permute-start.3 = (s32[1,1]{1,0:T(1,128)}, s32[1,1]{1,0:T(1,128)}, u32[]{:S(2)}, u32[]{:S(2)}) collective-permute-start(s32[1,1]{1,0:T(1,128)} %slice.58), channel_id=1, source_target_pairs={{0,1},{1,0},{2,3},{3,2},{4,5},{5,4},{6,7},{7,6},{8,9},{9,8},{10,11... | collective-permute-start | bytes 20 | tf_op jit(solution)/shard_map/ppermute | solution.py:184
where the time goes:
time: 90.8 us; the launch traced here: 90.2 us
  waiting for transfers between devices  28.7 us (32%)
  Pallas kernels  21.7 us (24%)
  blocking collectives  15 us (17%)
  starting transfers between devices  13.9 us (15%)
  between operations  3.89 us (4%)
  local copies, waits for them, and re-layouts  3.56 us (4%)
  other arithmetic  3.49 us (4%)
    all_to_all x2, waiting for transfers between devices, exchange(): lax.all_to_all(array, ('plane', 'wire'), split_axis=0, concat_axis=0, til...  27.6 us
    all_to_all x1, blocking collectives, exchange(): lax.all_to_all(array, ('plane', 'wire'), split_axis=0, concat_axis=0, til...  15 us
    pallas_call x1, Pallas kernels, convolve_inner(): pl.pallas_call(functools.partial(inner_kernel, tuple(chunks)), out_shape=...  10.7 us
    all_to_all x2, starting transfers between devices, exchange(): lax.all_to_all(array, ('plane', 'wire'), split_axis=0, concat_axis=0, til...  7.37 us
    ppermute x1, starting transfers between devices, wire_halo(): top = lax.ppermute(edge(slice(-PAD, None)), 'wire', up)  4.49 us
    pallas_call x1, Pallas kernels, convolve_edges(): pl.pallas_call(edge_kernel, out_shape=(jax.ShapeDtypeStruct((wires, ticks...  3.39 us
    pallas_call x1, Pallas kernels, make_image(): pl.pallas_call(functools.partial(image_kernel, owner_total, share), out_s...  2.69 us
    pallas_call x1, Pallas kernels, pack_tiles(): pl.pallas_call(functools.partial(pack_kernel, slots), out_shape=jax.Shape...  1.82 us
  transfers between devices with their start and end apart: 6, of which 3 were waited for; matrix products, arithmetic and copies ran while one was open for 4% of the time, Pallas kernels for 15%

commit v1 on v0

--- a/solution.py
+++ b/solution.py
@@ -10,6 +10,7 @@
 TB = 128
 CAP = 25
 PAD = 16
+TABLE = 8
 MIB = 1024 * 1024
 
 
@@ -447,9 +448,8 @@
             jnp.concatenate(chosen, axis=1),
             (((0,), (0,)), ((), ())),
             preferred_element_type=jnp.float32,
-        ).astype(jnp.bfloat16)
-        partial_ref[block] = sums[:, :TB]
-        partial_ref[block + 1] = sums[:, TB:]
+        )
+        partial_ref[:, block * TB : (block + 2) * TB] = sums
 
 
 def convolve_edges(plan, inner, raw, mask, left, right, top, bottom, bands, geometry):
@@ -463,7 +463,7 @@
         edge_kernel,
         out_shape=(
             jax.ShapeDtypeStruct((wires, ticks), jnp.bfloat16),
-            jax.ShapeDtypeStruct((blocks, cells, TB), jnp.bfloat16),
+            jax.ShapeDtypeStruct((cells, ticks), jnp.float32),
         ),
         in_specs=[smem()] + [vmem()] * 9,
         out_specs=(vmem(), vmem()),
@@ -478,8 +478,9 @@
     )(plan, inner, raw, mask, left, right, top, bottom, bands, geometry)
 
 
-def pack_kernel(slots, plan_ref, signal_ref, payload_ref, tiles_ref):
-    block_wires = payload_ref.shape[1]
+def pack_kernel(share, plan_ref, own_ref, signal_ref, payload_ref, tiles_ref):
+    owners, height, _ = payload_ref.shape
+    block_wires = (height - TABLE) // share
     wires, ticks = signal_ref.shape
     blocks = ticks // TB
     tiles_ref[...] = jnp.zeros_like(tiles_ref)
@@ -489,20 +490,29 @@
             tiles_ref[place] = signal_ref[
                 line * block_wires : (line + 1) * block_wires, block * TB : (block + 1) * TB
             ]
-    payload_ref[...] = tiles_ref[0:slots]
-
-
-def pack_tiles(plan, signal, slots, block_wires):
-    return pl.pallas_call(
-        functools.partial(pack_kernel, slots),
-        out_shape=jax.ShapeDtypeStruct((slots, block_wires, TB), jnp.bfloat16),
-        in_specs=[smem(), vmem()],
+    own = own_ref[...]
+    line = lax.broadcasted_iota(jnp.int32, (TABLE, 128), 0)
+    table = jnp.where(line == 0, own >> 7, jnp.where(line == 1, own & 127, 0))
+    table = table.astype(jnp.float32).astype(jnp.bfloat16)
+    for owner in range(owners):
+        payload_ref[owner, 0 : share * block_wires] = tiles_ref[
+            owner * share : (owner + 1) * share
+        ].reshape(share * block_wires, TB)
+        payload_ref[owner, share * block_wires : height] = table
+
+
+def pack_tiles(plan, own, signal, owner_total, share, block_wires):
+    height = share * block_wires + TABLE
+    return pl.pallas_call(
+        functools.partial(pack_kernel, share),
+        out_shape=jax.ShapeDtypeStruct((owner_total, height, TB), jnp.bfloat16),
+        in_specs=[smem(), vmem(), vmem()],
         out_specs=vmem(),
-        scratch_shapes=[pltpu.VMEM((slots + 1, block_wires, TB), jnp.bfloat16)],
+        scratch_shapes=[pltpu.VMEM((owner_total * share + 1, block_wires, TB), jnp.bfloat16)],
         cost_estimate=pl.CostEstimate(flops=10**8, bytes_accessed=3 * MIB, transcendentals=0),
         compiler_params=pltpu.CompilerParams(vmem_limit_bytes=8 * MIB),
         name="pack",
-    )(plan, signal)
+    )(plan, own, signal)
 
 
 def stage_kernel(slots, plan_ref, geo_ref, out_ref, rows_ref):
@@ -529,21 +539,18 @@
     )(plan, geometry)
 
 
-def image_kernel(owner_total, share, plan_ref, arrived_ref, staged_ref, image_ref, tiles_ref, sum_ref):
+def image_kernel(share, plan_ref, arrived_ref, staged_ref, busiest_ref, image_ref, tiles_ref, sum_ref):
     cells, ticks = image_ref.shape
     blocks = ticks // TB
-    block_wires = arrived_ref.shape[1]
+    owner_total, height, _ = arrived_ref.shape
+    block_wires = (height - TABLE) // share
     groups = staged_ref.shape[0]
     is_hot = plan_ref[1, 0] == plan_ref[1, 2]
     counts = plan_ref[1, 3] == 1
 
     @pl.when(is_hot)
     def _():
-        for source in range(owner_total):
-            sums = arrived_ref[source * share : source * share + cells // block_wires]
-            image_ref[:, source * TB : (source + 1) * TB] = sums.reshape(cells, TB).astype(
-                jnp.float32
-            )
+        image_ref[...] = busiest_ref[...]
 
     @pl.when(jnp.logical_not(is_hot))
     def _():
@@ -552,8 +559,11 @@
 
         @pl.when(counts)
         def _():
-            for slot in range(owner_total * share):
-                tiles_ref[plan_ref[0, slot]] = arrived_ref[slot]
+            for source in range(owner_total):
+                for slot in range(share):
+                    tiles_ref[plan_ref[0, source * share + slot]] = arrived_ref[
+                        source, slot * block_wires : (slot + 1) * block_wires
+                    ]
             for group in range(groups):
                 tiles = tiles_ref[group * GROUP : (group + 1) * GROUP]
                 sum_ref[plan_ref[3, group]] += jnp.dot(
@@ -566,13 +576,14 @@
             image_ref[:, block * TB : (block + 1) * TB] = sum_ref[block]
 
 
-def make_image(plan, arrived, staged, owner_total, share, ticks):
+def make_image(plan, arrived, staged, busiest, share):
     groups, cells, _ = staged.shape
-    block_wires = arrived.shape[1]
-    return pl.pallas_call(
-        functools.partial(image_kernel, owner_total, share),
+    block_wires = (arrived.shape[1] - TABLE) // share
+    ticks = busiest.shape[1]
+    return pl.pallas_call(
+        functools.partial(image_kernel, share),
         out_shape=jax.ShapeDtypeStruct((cells, ticks), jnp.float32),
-        in_specs=[smem(), vmem(), vmem()],
+        in_specs=[smem(), vmem(), vmem(), vmem()],
         out_specs=vmem(),
         scratch_shapes=[
             pltpu.VMEM((groups * GROUP + 1, block_wires, TB), jnp.bfloat16),
@@ -581,7 +592,7 @@
         cost_estimate=pl.CostEstimate(flops=10**8, bytes_accessed=3 * MIB, transcendentals=0),
         compiler_params=pltpu.CompilerParams(vmem_limit_bytes=16 * MIB),
         name="image",
-    )(plan, arrived, staged)
+    )(plan, arrived, staged, busiest)
 
 
 def more_kernel(owner_total, share, plan_ref, table_ref, arrived_ref, geo_ref, before_ref, image_ref):
@@ -720,29 +731,21 @@
         send_plan, inner, raw, mask, left, right, top, bottom, bands, geometry
     )
 
-    pieces = exchange(partial)
-    payload = pack_tiles(send_plan, signal, owner_total * share, block_wires)
-
-    payload, packed = lax.optimization_barrier((payload, packed))
-    rows = exchange(jnp.broadcast_to(packed[None], (owner_total, 1, 128)))[:, 0]
+    busiest = lax.psum(partial, ("plane", "wire"))
+    payload = pack_tiles(send_plan, packed, signal, owner_total, share, block_wires)
+    arrived = exchange(payload)
+
+    at = share * block_wires
+    rows = arrived[:, at].astype(jnp.int32) * 128 + arrived[:, at + 1].astype(jnp.int32)
     plan = make_receive_plan(
         rows, packed, owner_total, share, wires // block_wires, tick_blocks
     )
     staged = stage_geometry(
         plan, geometry, group_total(owner_total, share, tick_blocks), owner_total * share
     )
-
-    sums = jnp.sum(pieces.astype(jnp.float32), axis=0).astype(jnp.bfloat16)
-    payload = lax.dynamic_update_slice(
-        payload.reshape(owner_total, share, block_wires, TB),
-        sums.reshape(1, cells // block_wires, block_wires, TB),
-        (send_plan[1, 0], 0, 0, 0),
-    )
-    payload, facts = lax.optimization_barrier((payload, plan[1:2, 1:2]))
-    arrived = exchange(payload).reshape(owner_total * share, block_wires, TB)
-    image = make_image(plan, arrived, staged, owner_total, share, ticks)
-
-    trips = agree(facts)[0, 0]
+    image = make_image(plan, arrived, staged, busiest, share)
+
+    trips = agree(plan[1:2, 1:2])[0, 0]
     image = lax.fori_loop(
         0,
         trips,

time: 90.8 us -> 179 us (1.97)
  waiting for transfers between devices: 28.7 us -> 119 us
  blocking collectives: 15 us -> 0 us
  between operations: 3.89 us -> 15.5 us
    psum x0 -> x1, waiting for transfers between devices: none -> 87.8 us  [shards(): busiest = lax.psum(partial, ('plane', 'wire'))]
    all_to_all x1 -> x0, blocking collectives: 15 us -> none  [exchange(): lax.all_to_all(array, ('plane', 'wire'), split_axis=0, concat_axis=0, til...]
    unnamed x8 -> x16, local copies, waits for them, and re-layouts: 0.72 us -> 3.89 us
    all_to_all x2 -> x1, waiting for transfers between devices: 27.6 us -> 30.3 us  [exchange(): lax.all_to_all(array, ('plane', 'wire'), split_axis=0, concat_axis=0, til...]
    all_to_all x2 -> x1, starting transfers between devices: 7.37 us -> 7.93 us  [exchange(): lax.all_to_all(array, ('plane', 'wire'), split_axis=0, concat_axis=0, til...]
  transfers between devices with their start and end apart: 6 -> 6, of which waited for: 3 -> 2; matrix products, arithmetic and copies ran while one was open for 4% -> 1% of each run, Pallas kernels for 15% -> 10%
where the time goes in v1:
time: 179 us
  waiting for transfers between devices  119 us (66%)
  Pallas kernels  21.8 us (12%)
  between operations  15.5 us (9%)
  starting transfers between devices  14.4 us (8%)
  local copies, waits for them, and re-layouts  4.88 us (3%)
  other arithmetic  3.44 us (2%)
    psum x1, waiting for transfers between devices, shards(): busiest = lax.psum(partial, ('plane', 'wire'))  87.8 us
    all_to_all x1, waiting for transfers between devices, exchange(): lax.all_to_all(array, ('plane', 'wire'), split_axis=0, concat_axis=0, til...  30.3 us
    pallas_call x1, Pallas kernels, convolve_inner(): pl.pallas_call(functools.partial(inner_kernel, tuple(chunks)), out_shape=...  10.8 us
    all_to_all x1, starting transfers between devices, exchange(): lax.all_to_all(array, ('plane', 'wire'), split_axis=0, concat_axis=0, til...  7.93 us
    ppermute x1, starting transfers between devices, wire_halo(): top = lax.ppermute(edge(slice(-PAD, None)), 'wire', up)  4.49 us
    unnamed x16, local copies, waits for them, and re-layouts  3.89 us
  transfers between devices with their start and end apart: 6, of which 2 were waited for; matrix products, arithmetic and copies ran while one was open for 1% of the time, Pallas kernels for 10%

profile of v1, /device:TPU:0, one launch (start us, length us, event | category | flops | bytes accessed | tf_op | source)
XLA Modules:
  0.0 178.9 jit_solution(13917340816691348403)
XLA Ops:
  7.2 0.8 convert_element_type.19
  7.9 1.0 multiply_select_fusion
  8.9 0.5 collective-permute-start
  9.6 0.7 multiply_add_fusion
  10.4 1.0 slice_multiply_fusion
  11.4 0.4 send_plan.1.plan_ref
  11.8 0.7 copy-done.3
  12.5 0.6 bands.1.band_ref
  13.2 4.5 %collective-permute-start.1 = (bf16[16,2304]{1,0:T(8,128)(2,1)S(1)}, bf16[16,2304]{1,0:T(8,128)(2,1)S(1)}, u32[]{:S(2)}, u32[]{:S(2)}) collective-permute-start(bf16[16,2304]{1,0:T(8,128)(2,1)S(1)} %pad_maximum_fusion), channel_id=1, source_target_pairs={{0,2},{2,4},{4,6},{1,3},{3,5},{5,7},{8,10},{10,12},{12,14},{9,11},... | collective-permute-start | bytes 221192 | tf_op jit(solution)/shard_map/ppermute | solution.py:700
  17.7 1.4 collective-permute-start.2
  19.2 10.8 %inner.1.inner_ref = bf16[224,2048]{1,0:T(8,128)(2,1)S(1)} custom-call(bf16[256,2048]{1,0:T(8,128)(2,1)S(1)} %copy-done, bf16[256,1]{1,0:T(8,128)(2,1)S(1)} %convert_element_type.23.mask_ref, bf16[256,128]{1,0:T(8,128)(2,1)S(1)} %get-tuple-element.117.left_ref, bf16[256,128]{1,0:T(8,128)(2,1)S(1)} %get-tuple-element.116.right_ref, ...), custom_call_target="tpu_custom_call" | custom-call | flops 7751073792 | bytes 6291456 | tf_op jit(solution)/shard_map/inner/pallas_call | solution.py:342
  30.0 2.6 %edges.1 = (bf16[256,2048]{1,0:T(8,128)(2,1)S(1)}, f32[128,2048]{1,0:T(8,128)S(1)}) custom-call(s32[8,128]{1,0:T(8,128)S(1)} %send_plan.1.plan_ref, bf16[224,2048]{1,0:T(8,128)(2,1)S(1)} %inner.1.inner_ref, bf16[256,2048]{1,0:T(8,128)(2,1)S(1)} %copy-done, bf16[256,1]{1,0:T(8,128)(2,1)S(1)} %convert_element_type.23.mask_ref, ...), custom_call_target="tpu_custom_call" | custom-call | flops 1107296256 | bytes 6291456 | tf_op jit(solution)/shard_map/edges/pallas_call | solution.py:462
  32.6 1.0 copy-done.1
  33.6 1.0 copy-done.6
  34.6 1.9 %pack.1 = bf16[16,200,128]{2,1,0:T(8,128)(2,1)} custom-call(s32[8,128]{1,0:T(8,128)S(1)} %send_plan.1.plan_ref, s32[1,128]{1,0:T(1,128)S(1)} %get-tuple-element.203.own_ref, bf16[256,2048]{1,0:T(8,128)(2,1)S(1)} %get-tuple-element.201.signal_ref), custom_call_target="tpu_custom_call" | custom-call | flops 100000000 | bytes 3145728 | tf_op jit(solution)/shard_map/pack/pallas_call | solution.py:506
  36.4 7.9 %all-to-all-start.1 = ((bf16[16,200,128]{2,1,0:T(8,128)(2,1)}), bf16[16,200,128]{2,1,0:T(8,128)(2,1)S(1)}, u32[]{:S(2)}, u32[]{:S(2)}) async-start(bf16[16,200,128]{2,1,0:T(8,128)(2,1)} %pack.1), calls=%async_computation.1 | async-start | bytes 1638400 | tf_op jit(solution)/shard_map/all_to_all | solution.py:706
  44.5 0.7 all-reduce.3.cloned.1.call-update
  45.1 30.3 %all-to-all-done.1.arrived_ref = bf16[16,200,128]{2,1,0:T(8,128)(2,1)S(1)} async-done(((bf16[16,200,128]{2,1,0:T(8,128)(2,1)}), bf16[16,200,128]{2,1,0:T(8,128)(2,1)S(1)}, u32[]{:S(2)}, u32[]{:S(2)}) %all-to-all-start.1) | async-done | bytes 819232 | tf_op jit(solution)/shard_map/all_to_all | solution.py:706
  75.5 0.6 receive_plan.1.plan_ref
  76.2 0.6 slice.62
  76.8 2.1 %stage.1.staged_ref = bf16[26,128,256]{2,1,0:T(8,128)(2,1)S(1)} custom-call(s32[8,128]{1,0:T(8,128)S(1)} %receive_plan.1.plan_ref, bf16[128,32,128]{2,1,0:T(8,128)(2,1)} %geo_ref.3), custom_call_target="tpu_custom_call" | custom-call | flops 100000000 | bytes 3145728 | tf_op jit(solution)/shard_map/stage/pallas_call | solution.py:530
  78.9 87.8 %all-reduce.3.cloned.1.call-done.busiest_ref = f32[128,2048]{1,0:T(8,128)} async-done(((f32[128,2048]{1,0:T(8,128)}), f32[128,2048]{1,0:T(8,128)}) %all-reduce.3.cloned.1.call-update) | async-done | bytes 1048592 | tf_op jit(solution)/shard_map/psum | solution.py:734
  166.6 1.2 copy-done.2
  167.9 2.8 %image.1 = f32[128,2048]{1,0:T(8,128)} custom-call(s32[8,128]{1,0:T(8,128)S(1)} %receive_plan.1.plan_ref, bf16[16,200,128]{2,1,0:T(8,128)(2,1)S(1)} %all-to-all-done.1.arrived_ref, bf16[26,128,256]{2,1,0:T(8,128)(2,1)S(1)} %stage.1.staged_ref, f32[128,2048]{1,0:T(8,128)S(1)} %copy-done.2), custom_call_target="tpu_custom_call" | custom-call | flops 100000000 | bytes 3145728 | tf_op jit(solution)/shard_map/image/pallas_call | solution.py:583
  (29 shorter events, 0.6 us)
Async XLA Ops:
  7.2 12.0 %copy-start = (bf16[256,2048]{1,0:T(8,128)(2,1)S(1)}, bf16[256,2048]{1,0:T(8,128)(2,1)}, u32[]{:S(2)}) copy-start(bf16[256,2048]{1,0:T(8,128)(2,1)} %raw_ref.1) | copy-start | bytes 3145732
  8.9 4.2 %collective-permute-start = (bf16[256,128]{1,0:T(8,128)(2,1)S(1)}, bf16[256,128]{1,0:T(8,128)(2,1)S(1)}, u32[]{:S(2)}, u32[]{:S(2)}) collective-permute-start(bf16[256,128]{1,0:T(8,128)(2,1)S(1)} %multiply_select_fusion), channel_id=1, source_target_pairs={{0,1},{1,0},{2,3},{3,2},{4,5},{5,4},{6,7},{7,6},{8,9},{9,8},{10,11... | collective-permute-start | bytes 196616 | tf_op jit(solution)/shard_map/ppermute | solution.py:684
  11.8 0.7 copy-start.3
  13.2 16.8 %collective-permute-start.1 = (bf16[16,2304]{1,0:T(8,128)(2,1)S(1)}, bf16[16,2304]{1,0:T(8,128)(2,1)S(1)}, u32[]{:S(2)}, u32[]{:S(2)}) collective-permute-start(bf16[16,2304]{1,0:T(8,128)(2,1)S(1)} %pad_maximum_fusion), channel_id=1, source_target_pairs={{0,2},{2,4},{4,6},{1,3},{3,5},{5,7},{8,10},{10,12},{12,14},{9,11},... | collective-permute-start | bytes 221192 | tf_op jit(solution)/shard_map/ppermute | solution.py:700
  17.7 12.3 %copy-start.4 = (bf16[128,32,128]{2,1,0:T(8,128)(2,1)S(1)}, bf16[128,32,128]{2,1,0:T(8,128)(2,1)}, u32[]{:S(2)}) copy-start(bf16[128,32,128]{2,1,0:T(8,128)(2,1)} %geo_ref.3) | copy-start | bytes 3145732
  17.7 12.2 %collective-permute-start.2 = (bf16[16,2304]{1,0:T(8,128)(2,1)S(1)}, bf16[16,2304]{1,0:T(8,128)(2,1)S(1)}, u32[]{:S(2)}, u32[]{:S(2)}) collective-permute-start(bf16[16,2304]{1,0:T(8,128)(2,1)S(1)} %pad_maximum_fusion.1), channel_id=1, source_target_pairs={{2,0},{4,2},{6,4},{3,1},{5,3},{7,5},{10,8},{12,10},{14,12},{11,9},... | collective-permute-start | bytes 221192 | tf_op jit(solution)/shard_map/ppermute | solution.py:701
  32.6 1.0 copy-start.1
  33.6 1.0 copy-start.6
  36.4 39.0 %all-to-all-start.1 = ((bf16[16,200,128]{2,1,0:T(8,128)(2,1)}), bf16[16,200,128]{2,1,0:T(8,128)(2,1)S(1)}, u32[]{:S(2)}, u32[]{:S(2)}) async-start(bf16[16,200,128]{2,1,0:T(8,128)(2,1)} %pack.1), calls=%async_computation.1 | async-start | bytes 1638400 | tf_op jit(solution)/shard_map/all_to_all | solution.py:706
  44.4 127.6 %copy-start.7 = (s32[2]{0:T(128)S(1)}, s32[2]{0:T(128)}, u32[]{:S(2)}) copy-start(s32[2]{0:T(128)} %constant.110) | copy-start | bytes 28
  44.4 127.6 %copy-start.8 = (s32[2]{0:T(128)S(1)}, s32[2]{0:T(128)}, u32[]{:S(2)}) copy-start(s32[2]{0:T(128)} %constant.111) | copy-start | bytes 28
  44.4 122.2 %all-reduce.3.cloned.1.call-start = ((), (), s32[]{:S(2)}) async-start(), calls=%async_computation.2 | async-start | bytes 2097152 | tf_op jit(solution)/shard_map/psum | solution.py:734
  76.8 93.9 %collective-permute-start.3 = (s32[1,1]{1,0:T(1,128)}, s32[1,1]{1,0:T(1,128)}, u32[]{:S(2)}, u32[]{:S(2)}) collective-permute-start(s32[1,1]{1,0:T(1,128)} %slice.62), channel_id=1, source_target_pairs={{0,1},{1,0},{2,3},{3,2},{4,5},{5,4},{6,7},{7,6},{8,9},{9,8},{10,11... | collective-permute-start | bytes 20 | tf_op jit(solution)/shard_map/ppermute | solution.py:185
  166.6 1.2 copy-start.2
Sparse Core Ops, SparseCore 0:
  51.1 115.5 all-reduce.2
